TPU v7x, 256 devices: a whole 4x4x8 slice. The times are simulated.
256 devices in a mesh: layer: 4 (over z_lo, core), latent: 64 (over x, z_hi, y).
Axes of the slice: x: 4, y: 4, z: 8 (z_hi: 4, z_lo: 2; z = z_hi * 2 + z_lo), core: 2. Of those that a mesh axis runs over, the one named last changes fastest.
Arguments:
- acts: bfloat16 [4, 512, 2048], P('layer', None, 'latent'), may hold values from -6 to 6
- w_enc: bfloat16 [4, 2048, 32768], P('layer', None, 'latent'), may hold values from -0.0625 to 0.0625
- b_enc: float32 [32768], P('latent'), may hold values from -3 to 3
- w_dec: bfloat16 [4, 32768, 2048], P('layer', 'latent'), may hold values from -0.09375 to 0.09375
- b_dec: bfloat16 [4, 2048], P('layer', 'latent'), may hold values from -3 to 3
Outputs:
- grad_enc: bfloat16 [4, 2048, 32768], P('layer', None, 'latent')
- grad_dec: bfloat16 [4, 32768, 2048], P('layer', 'latent')
- grad_benc: float32 [32768], P('latent')
- grad_bdec: float32 [4, 2048], P('layer', 'latent')
All inputs are finite; a program needn't handle non-finite values.
Results may differ from a plain program's by a relative error of at most 0.014.
Values may be sent and summed in bfloat16 or wider, within the bound.
No kernel may reach another device: no remote copies, remote signals or barrier semaphores. Data moves between devices by JAX's collectives and lax.ppermute only.
A program may use at most 64 MiB of HBM per device.

v0:
```python
import jax
import jax.numpy as jnp
from jax import lax
from jax.sharding import Mesh
from jax.sharding import PartitionSpec as P

LATENT = ("latent_0", "latent_1", "latent_2")


def turned_gather(arrays, axis, dims):
    turned = [jnp.moveaxis(a, dim, 0) for a, dim in zip(arrays, dims)]
    widths = [t[0].size for t in turned]
    both = jnp.concatenate([t.reshape(-1, w) for t, w in zip(turned, widths)], axis=1)
    whole = lax.all_gather(both, axis, axis=0, tiled=True)
    blocks = jnp.split(whole, [sum(widths[:k]) for k in range(1, len(widths))], axis=1)
    return tuple(
        (
            jnp.moveaxis(b.reshape(-1, *t.shape[1:]), 0, dim)
            for b, t, dim in zip(blocks, turned, dims)
        )
    )


def sent_to_all(x, axis):
    peers = lax.axis_size(axis)
    return lax.all_to_all(jnp.broadcast_to(x[None], (peers, *x.shape)), axis, 0, 0, tiled=True)


def over_copies(x, axis):
    everything = sent_to_all(x, axis)
    return jnp.sum(everything, axis=0)


def sum_in_order(blocks, axes, order):
    inside = blocks.shape[1:]
    blocks = blocks.reshape(*(lax.axis_size(a) for a in axes), *inside)
    blocks = jnp.moveaxis(blocks, order, range(len(axes))).reshape(-1, *inside)
    for k in order:
        blocks = lax.psum_scatter(blocks, axes[k], scatter_dimension=0, tiled=True)
    return blocks[0]


def in_blocks(x, dim, peers):
    before, after = (x.shape[:dim], x.shape[dim + 1 :])
    return jnp.moveaxis(x.reshape(*before, peers, -1, *after), dim, 0)


def summed_rows(x, axes, order, dim):
    peers = lax.axis_size(axes)
    return sum_in_order(in_blocks(x, dim, peers), axes, order)


def taken_together(x, axis):
    everything = sent_to_all(x, axis)
    return jnp.sum(everything.astype(jnp.float32), axis=0)


def body(acts, w_enc, b_enc, w_dec, b_dec):
    local = acts[0]
    width_own = local.shape[1]
    enc_own = w_enc[0]
    dec_own = w_dec[0]
    full, bias_full = turned_gather((local, b_dec), LATENT, (1, 1))
    tokens_all = full.shape[0]
    scale = tokens_all ** (-0.5)
    part = jnp.dot(full, enc_own, preferred_element_type=jnp.float32)
    pre = over_copies(part, "layer") + b_enc[None, :]
    feat = (jax.nn.softplus(4.0 * pre) / 4.0).astype(jnp.bfloat16)
    rows = tokens_all // lax.axis_size(LATENT)
    recon = summed_rows(
        jnp.dot(feat, dec_own, preferred_element_type=jnp.float32), LATENT, (0, 2, 1), 0
    )
    position = lax.axis_index(LATENT)
    own_rows = lax.dynamic_slice_in_dim(full, position * rows, rows, 0)
    err_rows = (recon + bias_full.astype(jnp.float32) - own_rows.astype(jnp.float32)).astype(
        jnp.bfloat16
    )
    err = lax.all_gather(err_rows, LATENT, axis=0, tiled=True)
    bias_grad_full = scale * jnp.sum(err.astype(jnp.float32), axis=0)
    grad_bdec = lax.dynamic_slice_in_dim(bias_grad_full, position * width_own, width_own, 0)
    dec_prod = lax.dot_general(
        feat, err, (((0,), (0,)), ((), ())), preferred_element_type=jnp.float32
    )
    grad_dec = (scale * dec_prod).astype(jnp.bfloat16)
    feat_term = lax.dot_general(
        err, dec_own, (((1,), (1,)), ((), ())), preferred_element_type=jnp.float32
    )
    grad_feat = scale * taken_together(feat_term.astype(jnp.bfloat16), "layer").astype(jnp.float32)
    grad_pre = grad_feat * jax.nn.sigmoid(4.0 * pre)
    grad_benc = jnp.sum(grad_pre, axis=0)
    grad_pre_b = grad_pre.astype(jnp.bfloat16)
    enc_prod = lax.dot_general(
        full, grad_pre_b, (((0,), (0,)), ((), ())), preferred_element_type=jnp.float32
    )
    grad_enc = enc_prod.astype(jnp.bfloat16)
    return (grad_enc[None], grad_dec[None], grad_benc, grad_bdec[None])


def solution(mesh):
    finer = Mesh(
        mesh.devices.reshape(mesh.shape["layer"], 4, 4, 4),
        ("layer", "latent_0", "latent_1", "latent_2"),
    )
    placed = (
        P("layer", None, LATENT),
        P("layer", None, LATENT),
        P(LATENT),
        P("layer", LATENT, None),
        P("layer", LATENT),
    )
    return jax.shard_map(
        body,
        mesh=finer,
        in_specs=placed,
        out_specs=(
            P("layer", None, LATENT),
            P("layer", LATENT, None),
            P(LATENT),
            P("layer", LATENT),
        ),
        check_vma=False,
    )
```

profile of v0, /device:TPU:1, one launch (start us, length us, event | category | flops | bytes accessed | tf_op | source)
XLA Modules:
  0.0 392.8 jit_solution(11635537470442020400)
XLA Ops:
  7.2 0.0 copy-start
  7.2 0.0 all-gather.3.cloned.1.call-start
  7.2 0.9 copy.15
  8.1 1.4 pad_maximum_fusion
  9.5 0.0 all-gather.3.cloned.1.call-update
  9.5 0.0 reduce-scatter.4.cloned.1.call-start
  9.6 86.1 %all-gather.3.cloned.1.call-done = bf16[2048,513]{1,0:T(8,128)(2,1)} async-done(((bf16[32,513]{1,0:T(8,128)(2,1)}), bf16[2048,513]{1,0:T(8,128)(2,1)}) %all-gather.3.cloned.1.call-update) | async-done | bytes 2101264 | tf_op jit(solution)/shard_map/all_gather | solution.py:14
  95.7 3.5 fusion.5
  99.2 0.5 broadcast_in_dim.10
  99.7 52.5 %all_to_all.10 = f32[4,512,512]{2,1,0:T(8,128)} all-to-all(f32[4,512,512]{2,1,0:T(8,128)S(1)} %broadcast_in_dim.10), channel_id=1, replica_groups=mesh['layer'=4,'latent_0'=4,'latent_1'=4,'latent_2'=4] {'layer'}, dimensions={0} | all-to-all | bytes 8388608 | tf_op jit(solution)/shard_map/all_to_all | solution.py:26
  152.2 0.0 copy-start.4
  152.2 2.8 reduce_sum.36
  155.0 0.0 copy-done.4
  155.0 0.7 fusion.11
  155.8 0.0 copy-start.3
  155.8 0.8 copy-done.3
  156.6 0.0 copy-done
  156.6 1.2 convolution_bitcast_fusion
  157.8 2.2 copy.17
  160.0 0.0 reduce-scatter.4.cloned.1.call-update
  160.1 0.0 reduce-scatter.6.cloned.1.call-start
  160.1 47.6 %reduce-scatter.4.cloned.1.call-done = f32[16,8,2048]{2,1,0:T(8,128)} async-done(((f32[64,8,2048]{2,1,0:T(8,128)}), f32[16,8,2048]{2,1,0:T(8,128)}) %reduce-scatter.4.cloned.1.call-update) | async-done | bytes 1048592 | tf_op jit(solution)/shard_map/reduce_scatter | solution.py:39
  207.7 0.0 reduce-scatter.6.cloned.1.call-update
  207.7 0.0 reduce-scatter.8.cloned.1.call-start
  207.7 26.4 %reduce-scatter.6.cloned.1.call-done = f32[4,8,2048]{2,1,0:T(8,128)} async-done(((f32[16,8,2048]{2,1,0:T(8,128)}), f32[4,8,2048]{2,1,0:T(8,128)}) %reduce-scatter.6.cloned.1.call-update) | async-done | bytes 262160 | tf_op jit(solution)/shard_map/reduce_scatter | solution.py:39
  234.1 0.0 reduce-scatter.8.cloned.1.call-update
  234.2 0.0 all-gather.5.cloned.1.call-start
  234.2 0.0 slice-start
  234.2 1.6 slice-done
  235.8 1.0 constant_dynamic-slice_fusion
  236.8 1.2 copy.20
  238.0 1.3 convert_reduce_fusion.2
  239.3 22.5 %reduce-scatter.8.cloned.1.call-done = f32[1,8,2048]{2,1,0:T(8,128)} async-done(((f32[4,8,2048]{2,1,0:T(8,128)}), f32[1,8,2048]{2,1,0:T(8,128)}) %reduce-scatter.8.cloned.1.call-update) | async-done | bytes 65552 | tf_op jit(solution)/shard_map/reduce_scatter | solution.py:39
  261.8 1.5 fusion.13
  263.2 0.0 all-gather.5.cloned.1.call-update
  263.3 80.6 %all-gather.5.cloned.1.call-done = bf16[512,2048]{1,0:T(8,128)(2,1)} async-done(((bf16[8,2048]{1,0:T(8,128)(2,1)}), bf16[512,2048]{1,0:T(8,128)(2,1)}) %all-gather.5.cloned.1.call-update) | async-done | bytes 2097168 | tf_op jit(solution)/shard_map/all_gather | solution.py:78
  343.9 2.9 fusion.7
  346.8 1.5 broadcast_in_dim.11
  348.3 6.7 %all-to-all-start.1 = ((bf16[4,512,512]{2,1,0:T(8,128)(2,1)}), bf16[4,512,512]{2,1,0:T(8,128)(2,1)}, u32[]{:S(2)}, u32[]{:S(2)}) async-start(bf16[4,512,512]{2,1,0:T(8,128)(2,1)} %broadcast_in_dim.11), calls=%async_computation.4 | async-start | bytes 4194304 | tf_op jit(solution)/shard_map/all_to_all | solution.py:26
  355.0 0.0 copy-start.2
  355.0 2.1 convert_reduce_fusion
  357.1 0.6 fusion.14
  357.7 0.0 copy-done.2
  357.7 3.7 fusion.1
  361.3 18.6 %all-to-all-done.1 = bf16[4,512,512]{2,1,0:T(8,128)(2,1)} async-done(((bf16[4,512,512]{2,1,0:T(8,128)(2,1)}), bf16[4,512,512]{2,1,0:T(8,128)(2,1)}, u32[]{:S(2)}, u32[]{:S(2)}) %all-to-all-start.1) | async-done | bytes 2097184 | tf_op jit(solution)/shard_map/all_to_all | solution.py:26
  379.9 2.0 convert_reduce_fusion.1
  381.9 0.0 copy-start.1
  382.0 0.9 fusion.17
  382.9 0.8 copy-done.1
  383.7 2.6 fusion
Async XLA Ops:
  7.2 149.4 %copy-start = (bf16[1,512,2048]{2,1,0:T(8,128)(2,1)S(1)}, bf16[1,512,2048]{2,1,0:T(8,128)(2,1)}, u32[]{:S(2)}) copy-start(bf16[1,512,2048]{2,1,0:T(8,128)(2,1)} %param.8) | copy-start | bytes 6291460
  7.2 88.5 %all-gather.3.cloned.1.call-start = ((), (), s32[]{:S(2)}) async-start(), calls=%async_computation.5 | async-start | bytes 2662400 | tf_op jit(solution)/shard_map/all_gather | solution.py:14
  9.5 198.1 %reduce-scatter.4.cloned.1.call-start = ((), (), s32[]{:S(2)}) async-start(), calls=%async_computation.6 | async-start | bytes 5242880 | tf_op jit(solution)/shard_map/reduce_scatter | solution.py:39
  152.2 2.8 copy-start.4
  155.8 0.8 copy-start.3
  160.1 74.1 %reduce-scatter.6.cloned.1.call-start = ((), (), s32[]{:S(2)}) async-start(), calls=%async_computation.7 | async-start | bytes 1310720 | tf_op jit(solution)/shard_map/reduce_scatter | solution.py:39
  207.7 54.1 %reduce-scatter.8.cloned.1.call-start = ((), (), s32[]{:S(2)}) async-start(), calls=%async_computation.8 | async-start | bytes 327680 | tf_op jit(solution)/shard_map/reduce_scatter | solution.py:39
  234.2 109.7 %all-gather.5.cloned.1.call-start = ((), (), s32[]{:S(2)}) async-start(), calls=%async_computation.9 | async-start | bytes 2129920 | tf_op jit(solution)/shard_map/all_gather | solution.py:78
  234.2 1.6 slice-start
  348.3 31.7 %all-to-all-start.1 = ((bf16[4,512,512]{2,1,0:T(8,128)(2,1)}), bf16[4,512,512]{2,1,0:T(8,128)(2,1)}, u32[]{:S(2)}, u32[]{:S(2)}) async-start(bf16[4,512,512]{2,1,0:T(8,128)(2,1)} %broadcast_in_dim.11), calls=%async_computation.4 | async-start | bytes 4194304 | tf_op jit(solution)/shard_map/all_to_all | solution.py:26
  355.0 2.7 copy-start.2
  381.9 1.7 copy-start.1
Sparse Core Ops, SparseCore 0:
  11.9 83.7 all-gather.2
  160.2 47.4 reduce-scatter.3
  210.4 23.7 reduce-scatter.5
  236.5 25.2 reduce-scatter.7
  266.0 77.8 all-gather.4
where the time goes:
time: 393 us
  waiting for transfers between devices  282 us (72%)
  blocking collectives  52.5 us (13%)
  between operations  13.9 us (4%)
  matrix products  13.8 us (4%)
  other arithmetic  13.2 us (3%)
  local copies, waits for them, and re-layouts  10.5 us (3%)
  starting transfers between devices  6.93 us (2%)
    reduce_scatter x3, waiting for transfers between devices, sum_in_order(): blocks = lax.psum_scatter(blocks, axes[k], scatter_dimension=0, tiled=True)  96.4 us
    all_gather x1, waiting for transfers between devices, turned_gather(): whole = lax.all_gather(both, axis, axis=0, tiled=True)  86.1 us
    all_gather x1, waiting for transfers between devices, body(): err = lax.all_gather(err_rows, LATENT, axis=0, tiled=True)  80.6 us
    all_to_all x1, blocking collectives, sent_to_all(): lax.all_to_all(jnp.broadcast_to(x[None], (peers, *x.shape)), axis, 0, 0,...  52.5 us
    all_to_all x1, waiting for transfers between devices, sent_to_all(): lax.all_to_all(jnp.broadcast_to(x[None], (peers, *x.shape)), axis, 0, 0,...  18.6 us
  transfers between devices with their start and end apart: 6, of which 6 were waited for; matrix products, arithmetic and copies ran while one was open for 2% of the time, Pallas kernels for 0%

commit v1 on v0

--- a/solution.py
+++ b/solution.py
@@ -11,7 +11,9 @@
     turned = [jnp.moveaxis(a, dim, 0) for a, dim in zip(arrays, dims)]
     widths = [t[0].size for t in turned]
     both = jnp.concatenate([t.reshape(-1, w) for t, w in zip(turned, widths)], axis=1)
-    whole = lax.all_gather(both, axis, axis=0, tiled=True)
+    whole = jnp.concatenate(
+        lax.all_to_all(jnp.stack([both] * lax.axis_size(axis)), axis, 0, 0), axis=0
+    )
     blocks = jnp.split(whole, [sum(widths[:k]) for k in range(1, len(widths))], axis=1)
     return tuple(
         (

time: 393 us -> 572 us (1.46)
  waiting for transfers between devices: 282 us -> 371 us
  blocking collectives: 52.5 us -> 131 us
  local copies, waits for them, and re-layouts: 10.5 us -> 23.1 us
    reduce_scatter x3, waiting for transfers between devices: 96.4 us -> 277 us  [sum_in_order(): blocks = lax.psum_scatter(blocks, axes[k], scatter_dimension=0, tiled=True)]
    all_gather x1 -> x0, waiting for transfers between devices: 86.1 us -> none  [turned_gather(): whole = lax.all_gather(both, axis, axis=0, tiled=True)]
    all_to_all x0 -> x1, blocking collectives: none -> 76.2 us  [turned_gather(): lax.all_to_all(jnp.stack([both] * lax.axis_size(axis)), axis, 0, 0)]
    reduce_scatter x0 -> x1, local copies, waits for them, and re-layouts: none -> 9.8 us  [sum_in_order(): blocks = lax.psum_scatter(blocks, axes[k], scatter_dimension=0, tiled=True)]
  transfers between devices with their start and end apart: 6 -> 5, of which waited for: 6 -> 5; matrix products, arithmetic and copies ran while one was open for 2% -> 2% of each run, Pallas kernels for 0% -> 0%
where the time goes in v1:
time: 572 us; the launch traced here: 571 us
  waiting for transfers between devices  371 us (65%)
  blocking collectives  131 us (23%)
  local copies, waits for them, and re-layouts  23.1 us (4%)
  between operations  13.9 us (2%)
  other arithmetic  13.8 us (2%)
  matrix products  11.6 us (2%)
  starting transfers between devices  6.91 us (1%)
    reduce_scatter x3, waiting for transfers between devices, sum_in_order(): blocks = lax.psum_scatter(blocks, axes[k], scatter_dimension=0, tiled=True)  277 us
    all_to_all x1, blocking collectives, turned_gather(): lax.all_to_all(jnp.stack([both] * lax.axis_size(axis)), axis, 0, 0)  76.2 us
    all_gather x1, waiting for transfers between devices, body(): err = lax.all_gather(err_rows, LATENT, axis=0, tiled=True)  75.3 us
    all_to_all x1, blocking collectives, sent_to_all(): lax.all_to_all(jnp.broadcast_to(x[None], (peers, *x.shape)), axis, 0, 0,...  54.8 us
    all_to_all x1, waiting for transfers between devices, sent_to_all(): lax.all_to_all(jnp.broadcast_to(x[None], (peers, *x.shape)), axis, 0, 0,...  18.6 us
  transfers between devices with their start and end apart: 5, of which 5 were waited for; matrix products, arithmetic and copies ran while one was open for 2% of the time, Pallas kernels for 0%

profile of v1, /device:TPU:1, one launch (start us, length us, event | category | flops | bytes accessed | tf_op | source)
XLA Modules:
  0.0 571.5 jit_solution(752935282036041531)
XLA Ops:
  7.2 0.0 copy-start
  7.2 0.0 reduce-scatter.4.cloned.1.call-start
  7.2 0.9 copy.20
  8.1 0.8 pad_maximum_fusion
  8.9 0.2 stack.2
  9.1 0.0 copy-start.3
  9.1 76.2 %all_to_all.15 = bf16[64,32,513]{2,1,0:T(8,128)(2,1)S(1)} all-to-all(bf16[64,32,513]{2,1,0:T(8,128)(2,1)S(1)} %stack.2), channel_id=1, replica_groups=mesh['layer'=4,'latent_0'=4,'latent_1'=4,'latent_2'=4] {'latent_0','late..., dimensions={0} | all-to-all | bytes 4202496 | tf_op jit(solution)/shard_map/all_to_all | solution.py:15
  85.3 0.0 copy-start.1
  85.3 1.5 copy-done.1
  86.9 0.0 copy-done.3
  86.9 1.3 fusion.5
  88.1 0.5 broadcast_in_dim.10
  88.7 54.8 %all_to_all.16 = f32[4,512,512]{2,1,0:T(8,128)} all-to-all(f32[4,512,512]{2,1,0:T(8,128)S(1)} %broadcast_in_dim.10), channel_id=1, replica_groups=mesh['layer'=4,'latent_0'=4,'latent_1'=4,'latent_2'=4] {'layer'}, dimensions={0} | all-to-all | bytes 8388608 | tf_op jit(solution)/shard_map/all_to_all | solution.py:28
  143.4 0.0 copy-start.6
  143.4 2.8 reduce_sum.36
  146.2 0.0 copy-done.6
  146.2 0.7 fusion.11
  147.0 0.0 copy-start.5
  147.0 0.8 copy-done.5
  147.8 0.0 copy-done
  147.8 1.2 convolution_bitcast_fusion
  149.0 2.2 copy.21
  151.2 0.0 reduce-scatter.4.cloned.1.call-update
  151.3 0.0 reduce-scatter.6.cloned.1.call-start
  151.3 44.4 %reduce-scatter.4.cloned.1.call-done = f32[16,8,2048]{2,1,0:T(8,128)} async-done(((f32[64,8,2048]{2,1,0:T(8,128)}), f32[16,8,2048]{2,1,0:T(8,128)}) %reduce-scatter.4.cloned.1.call-update) | async-done | bytes 1048592 | tf_op jit(solution)/shard_map/reduce_scatter | solution.py:41
  195.7 9.8 %copy.22 = f32[16,8,2048]{1,2,0:T(8,128)} copy(f32[16,8,2048]{2,1,0:T(8,128)} %reduce-scatter.4.cloned.1.call-done) | data formatting | bytes 2097152 | tf_op jit(solution)/shard_map/reduce_scatter | solution.py:41
  205.5 0.0 reduce-scatter.6.cloned.1.call-update
  205.5 0.0 reduce-scatter.8.cloned.1.call-start
  205.5 150.4 %reduce-scatter.6.cloned.1.call-done = f32[4,8,2048]{1,2,0:T(8,128)} async-done(((f32[16,8,2048]{1,2,0:T(8,128)}), f32[4,8,2048]{1,2,0:T(8,128)}) %reduce-scatter.6.cloned.1.call-update) | async-done | bytes 262160 | tf_op jit(solution)/shard_map/reduce_scatter | solution.py:41
  355.9 0.0 reduce-scatter.8.cloned.1.call-update
  355.9 0.0 all-gather.2.cloned.1.call-start
  356.0 3.0 split.8
  359.0 1.3 convert_reduce_fusion.2
  360.3 82.5 %reduce-scatter.8.cloned.1.call-done = f32[1,8,2048]{1,2,0:T(8,128)} async-done(((f32[4,8,2048]{1,2,0:T(8,128)}), f32[1,8,2048]{1,2,0:T(8,128)}) %reduce-scatter.8.cloned.1.call-update) | async-done | bytes 65552 | tf_op jit(solution)/shard_map/reduce_scatter | solution.py:41
  442.8 2.6 bitcast_subtract_fusion
  445.4 1.8 copy.23
  447.2 0.0 all-gather.2.cloned.1.call-update
  447.3 75.3 %all-gather.2.cloned.1.call-done = bf16[512,2048]{1,0:T(8,128)(2,1)} async-done(((bf16[8,2048]{1,0:T(8,128)(2,1)}), bf16[512,2048]{1,0:T(8,128)(2,1)}) %all-gather.2.cloned.1.call-update) | async-done | bytes 2097168 | tf_op jit(solution)/shard_map/all_gather | solution.py:80
  522.5 2.9 fusion.7
  525.4 1.5 broadcast_in_dim.11
  526.9 6.7 %all-to-all-start.2 = ((bf16[4,512,512]{2,1,0:T(8,128)(2,1)}), bf16[4,512,512]{2,1,0:T(8,128)(2,1)}, u32[]{:S(2)}, u32[]{:S(2)}) async-start(bf16[4,512,512]{2,1,0:T(8,128)(2,1)} %broadcast_in_dim.11), calls=%async_computation.5 | async-start | bytes 4194304 | tf_op jit(solution)/shard_map/all_to_all | solution.py:28
  533.7 0.0 copy-start.4
  533.7 2.1 convert_reduce_fusion
  535.8 0.6 fusion.13
  536.4 0.0 copy-done.4
  536.4 3.7 fusion.1
  540.0 18.6 %all-to-all-done.2 = bf16[4,512,512]{2,1,0:T(8,128)(2,1)} async-done(((bf16[4,512,512]{2,1,0:T(8,128)(2,1)}), bf16[4,512,512]{2,1,0:T(8,128)(2,1)}, u32[]{:S(2)}, u32[]{:S(2)}) %all-to-all-start.2) | async-done | bytes 2097184 | tf_op jit(solution)/shard_map/all_to_all | solution.py:28
  558.6 2.0 convert_reduce_fusion.1
  560.6 0.0 copy-start.2
  560.6 0.9 fusion.16
  561.5 0.8 copy-done.2
  562.4 2.6 fusion
Async XLA Ops:
  7.2 140.6 %copy-start = (bf16[1,512,2048]{2,1,0:T(8,128)(2,1)S(1)}, bf16[1,512,2048]{2,1,0:T(8,128)(2,1)}, u32[]{:S(2)}) copy-start(bf16[1,512,2048]{2,1,0:T(8,128)(2,1)} %param.8) | copy-start | bytes 6291460
  7.2 188.5 %reduce-scatter.4.cloned.1.call-start = ((), (), s32[]{:S(2)}) async-start(), calls=%async_computation.6 | async-start | bytes 5242880 | tf_op jit(solution)/shard_map/reduce_scatter | solution.py:41
  9.1 77.8 %copy-start.3 = (bf16[1,2048,512]{2,1,0:T(8,128)(2,1)S(1)}, bf16[1,2048,512]{2,1,0:T(8,128)(2,1)}, u32[]{:S(2)}) copy-start(bf16[1,2048,512]{2,1,0:T(8,128)(2,1)} %param.6) | copy-start | bytes 6291460
  85.3 1.5 copy-start.1
  143.4 2.8 copy-start.6
  147.0 0.8 copy-start.5
  151.3 204.7 %reduce-scatter.6.cloned.1.call-start = ((), (), s32[]{:S(2)}) async-start(), calls=%async_computation.7 | async-start | bytes 20971520 | tf_op jit(solution)/shard_map/reduce_scatter | solution.py:41
  205.5 237.3 %reduce-scatter.8.cloned.1.call-start = ((), (), s32[]{:S(2)}) async-start(), calls=%async_computation.8 | async-start | bytes 5242880 | tf_op jit(solution)/shard_map/reduce_scatter | solution.py:41
  355.9 166.6 %all-gather.2.cloned.1.call-start = ((), (), s32[]{:S(2)}) async-start(), calls=%async_computation.9 | async-start | bytes 2129920 | tf_op jit(solution)/shard_map/all_gather | solution.py:80
  526.9 31.7 %all-to-all-start.2 = ((bf16[4,512,512]{2,1,0:T(8,128)(2,1)}), bf16[4,512,512]{2,1,0:T(8,128)(2,1)}, u32[]{:S(2)}, u32[]{:S(2)}) async-start(bf16[4,512,512]{2,1,0:T(8,128)(2,1)} %broadcast_in_dim.11), calls=%async_computation.5 | async-start | bytes 4194304 | tf_op jit(solution)/shard_map/all_to_all | solution.py:28
  533.7 2.7 copy-start.4
  560.6 1.7 copy-start.2
Sparse Core Ops, SparseCore 0:
  151.4 44.2 reduce-scatter.3
  205.6 150.2 reduce-scatter.5
  358.5 84.2 reduce-scatter.7
  447.4 75.1 all-gather.1
